TPU v7x, 128 devices: a whole 4x4x4 slice. The times are simulated.
128 devices in a mesh: rep: 16 (over z, x_hi, core), sec: 2 (over x_lo), mdl: 4 (over y).
Axes of the slice: x: 4 (x_hi: 2, x_lo: 2; x = x_hi * 2 + x_lo), y: 4, z: 4, core: 2. Of those that a mesh axis runs over, the one named last changes fastest.
Arguments:
- obs: bfloat16 [2, 8192, 1536], P('sec', 'rep'), may hold values from -6 to 6
- a_query: bfloat16 [1536, 1536], P(None, 'mdl'), may hold values from -0.15309311 to 0.15309311
- a_keyval: bfloat16 [2, 1536, 512], P(None, None, 'mdl'), may hold values from -0.15309311 to 0.15309311
- a_out: bfloat16 [1536, 1536], P('mdl'), may hold values from -0.15625 to 0.15625
- w_policy: bfloat16 [1536, 128], replicated, may hold values from -0.15625 to 0.15625
- c_in: bfloat16 [1536, 2048], P(None, 'mdl'), may hold values from -0.15309311 to 0.15309311
- c_query: bfloat16 [2048, 2048], P(None, 'mdl'), may hold values from -0.13258252 to 0.13258252
- c_keyval: bfloat16 [2, 2048, 512], P(None, None, 'mdl'), may hold values from -0.13258252 to 0.13258252
- c_out: bfloat16 [2048, 2048], P('mdl'), may hold values from -0.125 to 0.125
- w_value: bfloat16 [2048], replicated, may hold values from -0.110485435 to 0.110485435
- actions: int32 [2, 8192], P('sec', 'rep'), may hold values from 0 to 127
- advantages: float32 [2, 8192], P('sec', 'rep'), may hold values from -6 to 6
- old_logp: float32 [2, 8192], P('sec', 'rep'), may hold values from -7 to -4
- returns: float32 [2, 8192], P('sec', 'rep'), may hold values from -6 to 6
- robot_count: int32 [2], replicated, may hold values from 2048 to 8192, as said below
Outputs:
- values: float32 [2, 8192], P('sec', ('rep', 'mdl'))
- grad_a_out: float32 [1536, 1536], P('mdl')
- grad_c_out: float32 [2048, 2048], P('mdl')
Inputs may be any that keep to these rules, and one draw needn't show every extreme that they name: `robot_count`: one of the two micro-batches holds all 8192 robots, the other at least 2048; live robots are the first ones.
All inputs are finite; a program needn't handle non-finite values.
Results may differ from a plain program's by a relative error of at most 0.023.
Values may be sent and summed in bfloat16 or wider, within the bound.
A program may use at most 128 MiB of HBM per device.

v0:
```python
import math
import jax
import jax.numpy as jnp
from jax import lax
from jax.sharding import PartitionSpec as P

HEAD = 128
epsilon = 1e-05
clip_range = 0.2
masked_score = -1e30


def rms_normed(values_in):
    return values_in * lax.rsqrt(jnp.mean(values_in * values_in, axis=-1, keepdims=True) + epsilon)


def norm_backward(source, normed, grad_in):
    factor = lax.rsqrt(jnp.mean(source * source, axis=-1, keepdims=True) + epsilon)
    return factor * (grad_in - normed * jnp.mean(grad_in * normed, axis=-1, keepdims=True))


def project(source, w_query, w_keyval):
    normed = rms_normed(source).astype(jnp.bfloat16)
    queries = (
        jnp.dot(normed, w_query, preferred_element_type=jnp.float32) * HEAD ** (-0.5)
    ).astype(jnp.bfloat16)
    keyval = jnp.einsum("rd,cdk->crk", normed, w_keyval, preferred_element_type=jnp.float32).astype(
        jnp.bfloat16
    )
    return (queries, keyval)


def policy_backward(hidden, action_ids, advantage, old_values, live_mask, live_total, w_policy):
    source = hidden.astype(jnp.float32)
    normed = rms_normed(source)
    logits = jnp.dot(normed.astype(jnp.bfloat16), w_policy, preferred_element_type=jnp.float32)
    log_probs = jax.nn.log_softmax(logits, axis=-1)
    onehot = (action_ids[:, None] == lax.broadcasted_iota(jnp.int32, logits.shape, 1)).astype(
        jnp.float32
    )
    chosen = jnp.sum(onehot * log_probs, axis=-1)
    prob_ratio = jnp.exp(chosen - old_values)
    plain_term = prob_ratio * advantage
    bounded = jnp.clip(prob_ratio, 1.0 - clip_range, 1.0 + clip_range) * advantage
    slope_term = jnp.where(
        live_mask & (plain_term <= bounded), -plain_term / live_total, jnp.float32(0.0)
    )
    dlogits = slope_term[:, None] * (onehot - jnp.exp(log_probs))
    dnormed = jnp.dot(dlogits, w_policy.astype(jnp.float32).T, precision=lax.Precision.HIGHEST)
    return norm_backward(source, normed, dnormed)


def value_backward(mixed_out, target, live_mask, live_total, w_value):
    normed = rms_normed(mixed_out)
    value_pred = jnp.dot(normed.astype(jnp.bfloat16), w_value, preferred_element_type=jnp.float32)
    slope_term = jnp.where(live_mask, value_pred - target, jnp.float32(0.0)) / live_total
    dnormed = slope_term[:, None] * w_value.astype(jnp.float32)[None, :]
    return (value_pred, norm_backward(mixed_out, normed, dnormed))


def split_heads(queries, kv_heads):
    row_count = queries.shape[0]
    groups = queries.shape[1] // HEAD // kv_heads
    return queries.reshape(row_count, kv_heads, groups, HEAD)


def start_state(heads_in):
    row_count, kv_heads, groups, _ = heads_in.shape
    row_top = jnp.full((kv_heads, groups, row_count), masked_score, jnp.float32)
    row_sum = jnp.zeros((kv_heads, groups, row_count), jnp.float32)
    acc_sum = jnp.zeros((kv_heads, groups, row_count, HEAD), jnp.float32)
    return (row_top, row_sum, acc_sum)


def make_fold(heads_in, robot_total, carried, piece):
    kv_heads = heads_in.shape[1]
    piece_rows = piece.shape[1]
    block_rows = math.gcd(piece_rows, 512)
    block_count = piece_rows // block_rows
    key_blocks = piece[0].reshape(block_count, block_rows, kv_heads, HEAD)
    value_blocks = piece[1].reshape(block_count, block_rows, kv_heads, HEAD)

    def absorb(inner, block_item):
        block_index, key_block, value_block = block_item
        first_key = block_index * block_rows
        row_top, row_sum, acc_sum = inner
        scores = jnp.einsum(
            "rkgd,jkd->kgrj", heads_in, key_block, preferred_element_type=jnp.float32
        )
        key_live = first_key + lax.iota(jnp.int32, block_rows) < robot_total
        scores = jnp.where(key_live, scores, masked_score)
        new_top = jnp.maximum(row_top, jnp.max(scores, axis=-1))
        rescale = jnp.exp(row_top - new_top)
        weights = jnp.exp(scores - new_top[..., None])
        row_sum = row_sum * rescale + jnp.sum(weights, axis=-1)
        value_float = value_block.astype(jnp.float32)
        acc_sum = acc_sum * rescale[..., None] + jnp.einsum(
            "kgrj,jkd->kgrd", weights, value_float, precision=lax.Precision.HIGHEST
        )
        return ((new_top, row_sum, acc_sum), None)

    result, _ = lax.scan(
        absorb, carried, (jnp.arange(block_count, dtype=jnp.int32), key_blocks, value_blocks)
    )
    return result


def finish_heads(carried):
    _, row_sum, acc_sum = carried
    combined = acc_sum / row_sum[..., None]
    kv_heads, groups, row_count, _ = combined.shape
    return (
        jnp.transpose(combined, (2, 0, 1, 3))
        .reshape(row_count, kv_heads * groups * HEAD)
        .astype(jnp.bfloat16)
    )


def on_device(
    obs,
    a_query,
    a_keyval,
    a_out,
    w_policy,
    c_in,
    c_query,
    c_keyval,
    c_out,
    w_value,
    actions,
    advantages,
    old_logp,
    returns,
    robot_count,
):
    row_count = obs.shape[1]
    batch_index = lax.axis_index("sec")
    robot_total = robot_count[batch_index]
    live_total = jnp.sum(robot_count).astype(jnp.float32)
    first_row = lax.axis_index("rep") * row_count
    live_mask = first_row + lax.iota(jnp.int32, row_count) < robot_total
    mdl_count = lax.axis_size("mdl")
    part_rows = row_count // mdl_count
    row_start = lax.axis_index("mdl") * part_rows
    obs_float = obs[0].astype(jnp.float32)
    queries, keyval = project(obs_float, a_query, a_keyval)
    heads_a = split_heads(queries, keyval.shape[2] // HEAD)
    state_a = make_fold(
        heads_a,
        robot_total,
        start_state(heads_a),
        lax.all_gather(keyval, "rep", axis=1, tiled=True),
    )
    attended = finish_heads(state_a)
    mixed_sum = lax.psum(jnp.dot(attended, a_out, preferred_element_type=jnp.float32), "mdl")
    hidden = (obs_float + mixed_sum).astype(jnp.bfloat16)
    dhidden = policy_backward(
        hidden, actions[0], advantages[0], old_logp[0], live_mask, live_total, w_policy
    ).astype(jnp.bfloat16)
    actor_grad = jnp.einsum("rh,rd->hd", attended, dhidden, preferred_element_type=jnp.float32)
    embed_part = jnp.dot(hidden, c_in, preferred_element_type=jnp.float32).astype(jnp.bfloat16)
    embedded = lax.all_gather(embed_part, "mdl", axis=1, tiled=True)
    embed_float = embedded.astype(jnp.float32)
    critic_queries, critic_keyval = project(embed_float, c_query, c_keyval)
    heads_c = split_heads(critic_queries, critic_keyval.shape[2] // HEAD)
    state_c = make_fold(
        heads_c,
        robot_total,
        start_state(heads_c),
        lax.all_gather(critic_keyval, "rep", axis=1, tiled=True),
    )
    critic_attended = finish_heads(state_c)
    critic_sum = lax.psum(
        jnp.dot(critic_attended, c_out, preferred_element_type=jnp.float32).astype(jnp.bfloat16),
        "mdl",
    ).astype(jnp.float32)
    value_pred, dmixed = value_backward(
        embed_float + critic_sum, returns[0], live_mask, live_total, w_value
    )
    value_part = lax.dynamic_slice_in_dim(value_pred, row_start, part_rows, 0)
    dmixed_all = dmixed.astype(jnp.bfloat16)
    critic_grad = jnp.einsum(
        "rh,rd->hd", critic_attended, dmixed_all, preferred_element_type=jnp.float32
    )
    actor_summed, critic_summed = (
        lax.psum(actor_grad.astype(jnp.bfloat16), ("rep", "sec")).astype(jnp.float32),
        lax.psum(critic_grad.astype(jnp.bfloat16), ("rep", "sec")).astype(jnp.float32),
    )
    return (value_part[None, :], actor_summed, critic_summed)


def solution(mesh):
    return jax.shard_map(
        on_device,
        mesh=mesh,
        in_specs=(
            P("sec", "rep", None),
            P(None, "mdl"),
            P(None, None, "mdl"),
            P("mdl", None),
            P(),
            P(None, "mdl"),
            P(None, "mdl"),
            P(None, None, "mdl"),
            P("mdl", None),
            P(),
            P("sec", "rep"),
            P("sec", "rep"),
            P("sec", "rep"),
            P("sec", "rep"),
            P(),
        ),
        out_specs=(P("sec", ("rep", "mdl")), P("mdl", None), P("mdl", None)),
        check_vma=False,
    )
```

profile of v0, /device:TPU:1, one launch (start us, length us, event | category | flops | bytes accessed | tf_op | source)
XLA Modules:
  0.0 878.9 jit_solution(12537995733930431458)
XLA Ops:
  17.4 53.9 %all-gather.4.cloned.1.call-done = bf16[2,8192,128]{2,1,0:T(8,128)(2,1)} async-done(((bf16[2,512,128]{2,1,0:T(8,128)(2,1)}), bf16[2,8192,128]{2,1,0:T(8,128)(2,1)}) %all-gather.4.cloned.1.call-update) | async-done | bytes 4194320 | tf_op jit(solution)/shard_map/all_gather | solution.py:152
  75.9 188.8 %while.30 = (s32[]{:T(128)}, f32[1,3,512]{2,1,0:T(4,128)S(1)}, f32[1,3,512]{2,1,0:T(4,128)S(1)}, f32[1,3,512,128]{3,2,1,0:T(8,128)S(1)}, s32[16]{0:T(128)S(1)}, ...) while((s32[]{:T(128)}, f32[1,3,512]{2,1,0:T(4,128)S(1)}, ...), condition=%wide.region_4.5_spmd.clone, body=%wide.region_1.4_spmd.clone.sunk | while | flops 1415391232 | bytes 24348876 | solution.py:102
  271.0 73.2 %all-reduce.5.cloned.1.call-done = f32[512,1536]{1,0:T(8,128)} async-done(((f32[512,1536]{1,0:T(8,128)}), f32[512,1536]{1,0:T(8,128)}) %all-reduce.5.cloned.1.call-update) | async-done | bytes 3145744 | tf_op jit(solution)/shard_map/psum | solution.py:155
  350.9 30.8 %all-gather.6.cloned.1.call-done = bf16[512,2048]{1,0:T(8,128)(2,1)} async-done(((bf16[512,512]{1,0:T(8,128)(2,1)}), bf16[512,2048]{1,0:T(8,128)(2,1)}) %all-gather.6.cloned.1.call-update) | async-done | bytes 2097168 | tf_op jit(solution)/shard_map/all_gather | solution.py:162
  393.5 49.4 %all-gather.8.cloned.1.call-done = bf16[2,8192,128]{2,1,0:T(8,128)(2,1)} async-done(((bf16[2,512,128]{2,1,0:T(8,128)(2,1)}), bf16[2,8192,128]{2,1,0:T(8,128)(2,1)}) %all-gather.8.cloned.1.call-update) | async-done | bytes 4194320 | tf_op jit(solution)/shard_map/all_gather | solution.py:170
  447.4 234.7 %while.31 = (s32[]{:T(128)}, f32[1,4,512]{2,1,0:T(4,128)S(1)}, f32[1,4,512]{2,1,0:T(4,128)}, f32[1,4,512,128]{3,2,1,0:T(8,128)S(1)}, s32[16]{0:T(128)S(1)}, /*in...) while((s32[]{:T(128)}, f32[1,4,512]{2,1,0:T(4,128)S(1)}, ...), condition=%wide.region_10.11_spmd.clone, body=%wide.region_7.10_spmd.clone.sunk | while | flops 1887187968 | bytes 32447348 | solution.py:102
  457.1 4.9 fusion.153
  471.7 4.9 fusion.153
  486.4 4.9 fusion.153
  501.1 4.9 fusion.153
  515.7 4.9 fusion.153
  530.4 4.9 fusion.153
  545.1 4.9 fusion.153
  559.7 4.9 fusion.153
  574.4 4.9 fusion.153
  589.1 4.9 fusion.153
  603.8 4.9 fusion.153
  618.4 4.9 fusion.153
  633.1 4.9 fusion.153
  647.8 4.9 fusion.153
  662.4 4.9 fusion.153
  677.1 4.9 fusion.153
  691.4 52.2 %all-reduce.7.cloned.1.call-done = bf16[512,2048]{1,0:T(8,128)(2,1)} async-done(((bf16[512,2048]{1,0:T(8,128)(2,1)}), bf16[512,2048]{1,0:T(8,128)(2,1)}) %all-reduce.7.cloned.1.call-update) | async-done | bytes 2097168 | tf_op jit(solution)/shard_map/psum | solution.py:173
  757.4 109.0 %all-reduce.9.cloned.1.call-done = (bf16[384,1536]{1,0:T(8,128)(2,1)}, bf16[512,2048]{1,0:T(8,128)(2,1)}) async-done(((bf16[384,1536]{1,0:T(8,128)(2,1)}, bf16[512,2048]{1,0:T(8,128)(2,1)}), (bf16[384,1536]{1,0:T(8,128)(2,1)}, bf16[512,2048]{1,0:T(8,128)(2,1)})) %all-reduce.9.cloned.1.call-update) | async-done | bytes 3276816 | tf_op jit(solution)/shard_map/psum | solution.py:186
  (592 shorter events, 393.0 us)
Async XLA Ops:
  7.2 677.6 %copy-start = (bf16[512,2048]{1,0:T(8,128)(2,1)S(1)}, bf16[512,2048]{1,0:T(8,128)(2,1)}, u32[]{:S(2)}) copy-start(bf16[512,2048]{1,0:T(8,128)(2,1)} %param.27) | copy-start | bytes 6291460
  7.2 64.2 %all-gather.4.cloned.1.call-start = ((), (), s32[]{:S(2)}) async-start(), calls=%async_computation | async-start | bytes 4456448 | tf_op jit(solution)/shard_map/all_gather | solution.py:152
  12.1 332.1 %all-reduce.5.cloned.1.call-start = ((), (), s32[]{:S(2)}) async-start(), calls=%async_computation.1 | async-start | bytes 6291456 | tf_op jit(solution)/shard_map/psum | solution.py:155
  271.0 110.7 %all-gather.6.cloned.1.call-start = ((), (), s32[]{:S(2)}) async-start(), calls=%async_computation.2 | async-start | bytes 2621440 | tf_op jit(solution)/shard_map/all_gather | solution.py:162
  349.0 34.7 %copy-start.20 = (bf16[2,2048,128]{2,1,0:T(8,128)(2,1)S(1)}, bf16[2,2048,128]{2,1,0:T(8,128)(2,1)}, u32[]{:S(2)}) copy-start(bf16[2,2048,128]{2,1,0:T(8,128)(2,1)} %param.26) | copy-start | bytes 3145732
  350.8 92.0 %all-gather.8.cloned.1.call-start = ((), (), s32[]{:S(2)}) async-start(), calls=%async_computation.3 | async-start | bytes 4456448 | tf_op jit(solution)/shard_map/all_gather | solution.py:170
  386.8 356.8 %all-reduce.7.cloned.1.call-start = ((), (), s32[]{:S(2)}) async-start(), calls=%async_computation.4 | async-start | bytes 4194304 | tf_op jit(solution)/shard_map/psum | solution.py:173
  456.8 5.2 copy-start.10
  471.4 5.2 copy-start.10
  486.1 5.2 copy-start.10
  500.8 5.2 copy-start.10
  515.5 5.2 copy-start.10
  530.1 5.2 copy-start.10
  544.8 5.2 copy-start.10
  559.5 5.2 copy-start.10
  574.1 5.2 copy-start.10
  588.8 5.2 copy-start.10
  603.5 5.2 copy-start.10
  618.1 5.2 copy-start.10
  632.8 5.2 copy-start.10
  647.5 5.2 copy-start.10
  662.2 5.2 copy-start.10
  676.8 5.2 copy-start.10
  687.4 179.0 %all-reduce.9.cloned.1.call-start = ((), (), s32[]{:S(2)}) async-start(), calls=%async_computation.5 | async-start | bytes 6553600 | tf_op jit(solution)/shard_map/psum | solution.py:186
  (127 other events, 366.8 us)
Sparse Core Ops, SparseCore 0:
  12.2 59.0 all-gather.3
  271.1 73.0 all-reduce.4
  350.9 30.6 all-gather.5
  386.9 55.8 all-gather.7
  687.5 56.0 all-reduce.6
  756.9 109.4 all-reduce.8
where the time goes:
time: 881 us; the launch traced here: 879 us
  waiting for transfers between devices  369 us (42%)
  matrix products  286 us (32%)
  other arithmetic  135 us (15%)
  local copies, waits for them, and re-layouts  50.4 us (6%)
  loops' own time  23.5 us (3%)
  between operations  15.1 us (2%)
    dot_general x32, matrix products, absorb(): jnp.einsum('kgrj,jkd->kgrd', weights, value_float, precision=lax.Precisio...  142 us
    dot_general x32, matrix products, absorb(): jnp.einsum('rkgd,jkd->kgrj', heads_in, key_block, preferred_element_type=...  112 us
    psum x1, waiting for transfers between devices, on_device(): lax.psum(actor_grad.astype(jnp.bfloat16), ('rep', 'sec'))  109 us
    reduce_sum x32, other arithmetic, absorb(): row_sum = row_sum * rescale + jnp.sum(weights, axis=-1)  92.6 us
    psum x1, waiting for transfers between devices, on_device(): lax.psum(jnp.dot(attended, a_out, preferred_element_type=jnp.float32), 'm...  73.2 us
    all_gather x1, waiting for transfers between devices, on_device(): lax.all_gather(keyval, 'rep', axis=1, tiled=True)  53.9 us
    psum x1, waiting for transfers between devices, on_device(): lax.psum(jnp.dot(critic_attended, c_out, preferred_element_type=jnp.float...  52.2 us
    all_gather x1, waiting for transfers between devices, on_device(): lax.all_gather(critic_keyval, 'rep', axis=1, tiled=True)  49.4 us
  transfers between devices with their start and end apart: 6, of which 6 were waited for; matrix products, arithmetic and copies ran while one was open for 2% of the time, Pallas kernels for 0%

commit v1 on v0

--- a/solution.py
+++ b/solution.py
@@ -183,7 +183,9 @@
         "rh,rd->hd", critic_attended, dmixed_all, preferred_element_type=jnp.float32
     )
     actor_summed, critic_summed = (
-        lax.psum(actor_grad.astype(jnp.bfloat16), ("rep", "sec")).astype(jnp.float32),
+        jnp.sum(lax.all_gather(actor_grad.astype(jnp.bfloat16), ("rep", "sec")), axis=0).astype(
+            jnp.float32
+        ),
         lax.psum(critic_grad.astype(jnp.bfloat16), ("rep", "sec")).astype(jnp.float32),
     )
     return (value_part[None, :], actor_summed, critic_summed)

time: 881 us -> 964 us (1.094)
  waiting for transfers between devices: 369 us -> 566 us
  matrix products: 286 us -> 229 us
  other arithmetic: 135 us -> 78.7 us
    all_gather x0 -> x1, waiting for transfers between devices: none -> 206 us  [on_device(): lax.all_gather(actor_grad.astype(jnp.bfloat16), ('rep', 'sec'))]
    reduce_sum x32, other arithmetic: 92.6 us -> 22.1 us  [absorb(): row_sum = row_sum * rescale + jnp.sum(weights, axis=-1)]
    dot_general x32, matrix products: 112 us -> 53.4 us  [absorb(): jnp.einsum('rkgd,jkd->kgrj', heads_in, key_block, preferred_element_type=...]
    while x288 -> x32, local copies, waits for them, and re-layouts: 14.1 us -> 0.09 us
    reduce_sum x0 -> x1, other arithmetic: none -> 13 us  [on_device(): jnp.sum(lax.all_gather(actor_grad.astype(jnp.bfloat16), ('rep', 'sec')),...]
    dynamic_slice x32, local copies, waits for them, and re-layouts: 18.8 us -> 30.8 us  [make_fold(): lax.scan(absorb, carried, (jnp.arange(block_count, dtype=jnp.int32), key_...]
  transfers between devices with their start and end apart: 6 -> 7, of which waited for: 6 -> 7; matrix products, arithmetic and copies ran while one was open for 2% -> 3% of each run, Pallas kernels for 0% -> 0%
where the time goes in v1:
time: 964 us; the launch traced here: 961 us
  waiting for transfers between devices  566 us (59%)
  matrix products  229 us (24%)
  other arithmetic  78.7 us (8%)
  local copies, waits for them, and re-layouts  49.5 us (5%)
  loops' own time  21.9 us (2%)
  between operations  15.1 us (2%)
    all_gather x1, waiting for transfers between devices, on_device(): lax.all_gather(actor_grad.astype(jnp.bfloat16), ('rep', 'sec'))  206 us
    dot_general x32, matrix products, absorb(): jnp.einsum('kgrj,jkd->kgrd', weights, value_float, precision=lax.Precisio...  142 us
    psum x1, waiting for transfers between devices, on_device(): lax.psum(critic_grad.astype(jnp.bfloat16), ('rep', 'sec'))  100 us
    psum x1, waiting for transfers between devices, on_device(): lax.psum(jnp.dot(attended, a_out, preferred_element_type=jnp.float32), 'm...  73.2 us
    all_gather x1, waiting for transfers between devices, on_device(): lax.all_gather(keyval, 'rep', axis=1, tiled=True)  53.9 us
    dot_general x32, matrix products, absorb(): jnp.einsum('rkgd,jkd->kgrj', heads_in, key_block, preferred_element_type=...  53.4 us
    psum x1, waiting for transfers between devices, on_device(): lax.psum(jnp.dot(critic_attended, c_out, preferred_element_type=jnp.float...  52.2 us
    all_gather x1, waiting for transfers between devices, on_device(): lax.all_gather(critic_keyval, 'rep', axis=1, tiled=True)  49.3 us
  transfers between devices with their start and end apart: 7, of which 7 were waited for; matrix products, arithmetic and copies ran while one was open for 3% of the time, Pallas kernels for 0%

profile of v1, /device:TPU:1, one launch (start us, length us, event | category | flops | bytes accessed | tf_op | source)
XLA Modules:
  0.0 961.0 jit_solution(685229532629185302)
XLA Ops:
  17.4 53.9 %all-gather.6.cloned.1.call-done = bf16[2,8192,128]{2,1,0:T(8,128)(2,1)} async-done(((bf16[2,512,128]{2,1,0:T(8,128)(2,1)}), bf16[2,8192,128]{2,1,0:T(8,128)(2,1)}) %all-gather.6.cloned.1.call-update) | async-done | bytes 4194320 | tf_op jit(solution)/shard_map/all_gather | solution.py:152
  75.9 129.9 %while.30 = (s32[]{:T(128)}, f32[1,3,512]{2,1,0:T(4,128)S(1)}, f32[1,3,512]{2,1,0:T(4,128)S(1)}, f32[1,3,512,128]{3,2,1,0:T(8,128)S(1)}, s32[16]{0:T(128)S(1)}, ...) while((s32[]{:T(128)}, f32[1,3,512]{2,1,0:T(4,128)S(1)}, ...), condition=%wide.region_4.5_spmd.clone, body=%wide.region_1.4_spmd.clone.sunk | while | flops 1415391232 | bytes 11765937 | solution.py:102
  212.1 73.2 %all-reduce.4.cloned.1.call-done = f32[512,1536]{1,0:T(8,128)} async-done(((f32[512,1536]{1,0:T(8,128)}), f32[512,1536]{1,0:T(8,128)}) %all-reduce.4.cloned.1.call-update) | async-done | bytes 3145744 | tf_op jit(solution)/shard_map/psum | solution.py:155
  291.9 30.8 %all-gather.8.cloned.1.call-done = bf16[512,2048]{1,0:T(8,128)(2,1)} async-done(((bf16[512,512]{1,0:T(8,128)(2,1)}), bf16[512,2048]{1,0:T(8,128)(2,1)}) %all-gather.8.cloned.1.call-update) | async-done | bytes 2097168 | tf_op jit(solution)/shard_map/all_gather | solution.py:162
  335.1 49.3 %all-gather.10.cloned.1.call-done = bf16[2,8192,128]{2,1,0:T(8,128)(2,1)} async-done(((bf16[2,512,128]{2,1,0:T(8,128)(2,1)}), bf16[2,8192,128]{2,1,0:T(8,128)(2,1)}) %all-gather.10.cloned.1.call-update) | async-done | bytes 4194320 | tf_op jit(solution)/shard_map/all_gather | solution.py:170
  389.5 161.6 %while.31 = (s32[]{:T(128)}, f32[1,4,512]{2,1,0:T(4,128)S(1)}, f32[1,4,512]{2,1,0:T(4,128)S(1)}, f32[1,4,512,128]{3,2,1,0:T(8,128)S(1)}, s32[16]{0:T(128)}, /*in...) while((s32[]{:T(128)}, f32[1,4,512]{2,1,0:T(4,128)S(1)}, ...), condition=%wide.region_10.11_spmd.clone, body=%wide.region_7.10_spmd.clone.sunk | while | flops 1887187968 | bytes 15599793 | solution.py:102
  394.6 4.9 fusion.153
  404.7 4.9 fusion.153
  414.9 4.9 fusion.153
  425.0 4.9 fusion.153
  435.1 4.9 fusion.153
  445.2 4.9 fusion.153
  455.3 4.9 fusion.153
  465.4 4.9 fusion.153
  475.5 4.9 fusion.153
  485.6 4.9 fusion.153
  495.7 4.9 fusion.153
  526.0 4.9 fusion.153
  536.1 4.9 fusion.153
  546.2 4.9 fusion.153
  560.5 52.2 %all-reduce.6.cloned.1.call-done = bf16[512,2048]{1,0:T(8,128)(2,1)} async-done(((bf16[512,2048]{1,0:T(8,128)(2,1)}), bf16[512,2048]{1,0:T(8,128)(2,1)}) %all-reduce.6.cloned.1.call-update) | async-done | bytes 2097168 | tf_op jit(solution)/shard_map/psum | solution.py:173
  628.9 100.4 %all-reduce.8.cloned.1.call-done = bf16[512,2048]{1,0:T(8,128)(2,1)} async-done(((bf16[512,2048]{1,0:T(8,128)(2,1)}), bf16[512,2048]{1,0:T(8,128)(2,1)}) %all-reduce.8.cloned.1.call-update) | async-done | bytes 2097168 | tf_op jit(solution)/shard_map/psum | solution.py:189
  733.4 206.2 %all-gather.12.cloned.1.call-done = bf16[12288,1536]{1,0:T(8,128)(2,1)} async-done(((bf16[384,1536]{1,0:T(8,128)(2,1)}), bf16[12288,1536]{1,0:T(8,128)(2,1)}) %all-gather.12.cloned.1.call-update) | async-done | bytes 37748752 | tf_op jit(solution)/shard_map/all_gather | solution.py:186
  939.5 13.0 %reduce_sum.132 = bf16[384,1536]{1,0:T(8,128)(2,1)S(1)} reduce(bf16[32,384,1536]{2,1,0:T(8,128)(2,1)} %bitcast.266, bf16[]{:T(256)} %constant.92.clone.1), dimensions={0}, to_apply=%region_19.20 | reduce | flops 18284544 | bytes 38928384 | tf_op jit(solution)/shard_map/reduce_sum | solution.py:186
  (339 shorter events, 276.1 us)
Async XLA Ops:
  7.2 546.7 %copy-start = (bf16[512,2048]{1,0:T(8,128)(2,1)S(1)}, bf16[512,2048]{1,0:T(8,128)(2,1)}, u32[]{:S(2)}) copy-start(bf16[512,2048]{1,0:T(8,128)(2,1)} %param.27) | copy-start | bytes 6291460
  7.2 64.2 %all-gather.6.cloned.1.call-start = ((), (), s32[]{:S(2)}) async-start(), calls=%async_computation | async-start | bytes 4456448 | tf_op jit(solution)/shard_map/all_gather | solution.py:152
  12.1 4.7 copy-start.14
  12.1 273.2 %all-reduce.4.cloned.1.call-start = ((), (), s32[]{:S(2)}) async-start(), calls=%async_computation.1 | async-start | bytes 6291456 | tf_op jit(solution)/shard_map/psum | solution.py:155
  212.1 110.6 %all-gather.8.cloned.1.call-start = ((), (), s32[]{:S(2)}) async-start(), calls=%async_computation.2 | async-start | bytes 2621440 | tf_op jit(solution)/shard_map/all_gather | solution.py:162
  285.3 4.7 copy-start.12
  288.9 1.1 copy-start.2
  290.1 35.3 %copy-start.13 = (bf16[2,2048,128]{2,1,0:T(8,128)(2,1)S(1)}, bf16[2,2048,128]{2,1,0:T(8,128)(2,1)}, u32[]{:S(2)}) copy-start(bf16[2,2048,128]{2,1,0:T(8,128)(2,1)} %param.26) | copy-start | bytes 3145732
  291.9 92.6 %all-gather.10.cloned.1.call-start = ((), (), s32[]{:S(2)}) async-start(), calls=%async_computation.3 | async-start | bytes 4456448 | tf_op jit(solution)/shard_map/all_gather | solution.py:170
  324.8 0.6 copy-start.10
  328.4 284.3 %all-reduce.6.cloned.1.call-start = ((), (), s32[]{:S(2)}) async-start(), calls=%async_computation.4 | async-start | bytes 4194304 | tf_op jit(solution)/shard_map/psum | solution.py:173
  553.8 2.9 copy-start.15
  553.9 3.6 copy-start.5
  553.9 4.2 copy-start.7
  556.5 3.9 copy-start.6
  556.5 172.7 %all-reduce.8.cloned.1.call-start = ((), (), s32[]{:S(2)}) async-start(), calls=%async_computation.5 | async-start | bytes 4194304 | tf_op jit(solution)/shard_map/psum | solution.py:189
  612.7 3.2 copy-start.1
  612.7 3.5 copy-start.4
  615.8 1.2 copy-start.11
  618.7 3.2 copy-start.8
  618.8 3.2 copy-start.9
  621.8 317.7 %all-gather.12.cloned.1.call-start = ((), (), s32[]{:S(2)}) async-start(), calls=%async_computation.6 | async-start | bytes 38928384 | tf_op jit(solution)/shard_map/all_gather | solution.py:186
  621.9 4.4 copy-start.3
Sparse Core Ops, SparseCore 0:
  12.2 59.0 all-gather.5
  212.2 73.0 all-reduce.3
  292.0 30.6 all-gather.7
  328.5 55.8 all-gather.9
  556.6 56.0 all-reduce.5
  622.0 107.2 all-reduce.7
  731.0 208.4 all-gather.11
